TPU v7x, 256 devices: a whole 4x4x8 slice. The times are simulated.
256 devices in a mesh: ctx: 64 (over x_hi, y, z), tp: 4 (over x_lo, core).
Axes of the slice: x: 4 (x_hi: 2, x_lo: 2; x = x_hi * 2 + x_lo), y: 4, z: 8, core: 2. Of those that a mesh axis runs over, the one named last changes fastest.
Arguments:
- queries: bfloat16 [16384, 4096], P('ctx', 'tp'), may hold values from -6 to 6
- keys: bfloat16 [16384, 512], P('ctx', 'tp'), may hold values from -6 to 6
- values: bfloat16 [16384, 512], P('ctx', 'tp'), may hold values from -6 to 6
- outputs: bfloat16 [16384, 4096], P('ctx', 'tp'), may hold values from -4 to 4
- grad_out: bfloat16 [16384, 4096], P('ctx', 'tp'), may hold values from -4 to 4
- log_sums: float32 [32, 16384], P('tp', 'ctx'), may hold values from 1.5 to 3.5
- block_mask: int32 [64, 3], P('ctx'), may hold values from 0 to 1, as said below
- grad_tokens: bfloat16 [16384, 4096], P('ctx', 'tp'), may hold values from -6 to 6
- expert_ids: int32 [16384, 2], P('ctx'), may hold values from 0 to 63, all different within a row; in each aligned block of 256 rows (0 to 255, 256 to 511, ...) at most 16 rows name the same one
- route_probs: float32 [16384, 2], P('ctx'), may hold values from 0.05 to 0.6
- hidden_saved: bfloat16 [64, 1024, 1536], P('ctx', None, 'tp'), may hold values from -6 to 6
- down_weight: bfloat16 [64, 1536, 4096], P('ctx', None, 'tp'), may hold values from -0.15625 to 0.15625
Outputs:
- grad_queries: bfloat16 [16384, 4096], P('ctx', 'tp')
- grad_keys: bfloat16 [16384, 512], P('ctx', 'tp')
- grad_values: bfloat16 [16384, 512], P('ctx', 'tp')
- grad_weight: bfloat16 [64, 1536, 4096], P('ctx', None, 'tp')
- grad_hidden: bfloat16 [64, 1536, 1024], P('ctx', 'tp')
Inputs may be any that keep to these rules, and one draw needn't show every extreme that they name: `expert_ids`: among the routes of one block of 256 tokens, no expert is named more than 16 times, a bound that some block reaches; a token names 2 different experts. block_mask[r, r - 1] = 1 for r = 1 .. 3: block r attends the first block.
All inputs are finite; a program needn't handle non-finite values.
Results may differ from a plain program's by a relative error of at most 0.0052.
Values may be sent and summed in bfloat16 or wider, within the bound.
A program may use at most 128 MiB of HBM per device.

v0:
```python
import jax
import jax.numpy as jnp
from jax import lax
from jax.sharding import PartitionSpec as P

HD = 128
WIN = 4


def shifted(x, axis, by):
    devices = lax.axis_size(axis)
    pairs = [(i, i + by) for i in range(devices) if 0 <= i + by < devices]
    return lax.ppermute(x, axis, pairs)


def passed_along(block, axis, distance):
    devices = range(lax.axis_size(axis))
    route = [((i - distance) % len(devices), i) for i in devices]
    return lax.ppermute(block, axis, route)


def dispatch_rows(grad_rows, expert_ids, route_probs, expert_count, capacity):
    top_count = expert_ids.shape[1]
    route_count = expert_ids.shape[0] * top_count
    flat_ids = expert_ids.reshape(-1)
    one_hot = (flat_ids[:, None] == jnp.arange(expert_count, dtype=jnp.int32)[None, :]).astype(
        jnp.int32
    )
    earlier = jnp.cumsum(one_hot, axis=0, dtype=jnp.int32) - one_hot
    slot_index = jnp.sum(earlier * one_hot, axis=1, dtype=jnp.int32)
    target = flat_ids * capacity + slot_index
    source = (
        jnp.zeros((expert_count * capacity,), jnp.int32)
        .at[target]
        .set(jnp.arange(route_count, dtype=jnp.int32) + 1)
    )
    chosen = jnp.maximum(source - 1, 0)
    factor = jnp.where(source > 0, route_probs.reshape(-1)[chosen], 0.0)
    picked = grad_rows[chosen // top_count].astype(jnp.float32) * factor[:, None]
    return picked.astype(jnp.bfloat16).reshape(expert_count, capacity, grad_rows.shape[1])


def shards(
    queries,
    keys,
    values,
    outputs,
    grad_out,
    log_sums,
    block_mask,
    grad_tokens,
    expert_ids,
    route_probs,
    hidden_saved,
    down_weight,
):
    tokens_here = queries.shape[0]
    kv_local = keys.shape[1] // HD
    groups = queries.shape[1] // HD // kv_local
    score_scale = HD ** (-0.5)
    query_heads = queries.reshape(tokens_here, kv_local, groups, HD)
    grad_heads = grad_out.reshape(tokens_here, kv_local, groups, HD)
    output_heads = outputs.reshape(tokens_here, kv_local, groups, HD)
    delta_rows = jnp.sum(
        grad_heads.astype(jnp.float32) * output_heads.astype(jnp.float32), axis=-1
    ).transpose(1, 2, 0)
    log_heads = log_sums.reshape(kv_local, groups, tokens_here)
    key_block = keys.reshape(tokens_here, kv_local, HD)
    value_block = values.reshape(tokens_here, kv_local, HD)
    position = lax.axis_index("ctx")
    causal = jnp.tril(jnp.ones((tokens_here, tokens_here), jnp.float32))

    def block_terms(key_rows, value_rows, live_flag):
        scores = (
            jnp.einsum("tkgd,ukd->kgtu", query_heads, key_rows, preferred_element_type=jnp.float32)
            * score_scale
        )
        weights = jnp.exp(scores - log_heads[..., None]) * live_flag
        weights_low = weights.astype(jnp.bfloat16)
        value_term = jnp.einsum(
            "kgtu,tkgd->ukd", weights_low, grad_heads, preferred_element_type=jnp.float32
        )
        grad_weights = jnp.einsum(
            "tkgd,ukd->kgtu", grad_heads, value_rows, preferred_element_type=jnp.float32
        )
        grad_scores = (weights * (grad_weights - delta_rows[..., None])).astype(jnp.bfloat16)
        query_term = (
            jnp.einsum("kgtu,ukd->tkgd", grad_scores, key_rows, preferred_element_type=jnp.float32)
            * score_scale
        )
        key_term = (
            jnp.einsum(
                "kgtu,tkgd->ukd", grad_scores, query_heads, preferred_element_type=jnp.float32
            )
            * score_scale
        )
        return (query_term, key_term, value_term)

    query_term, key_own, value_own = block_terms(key_block, value_block, causal)
    grad_query = query_term
    home_keys, home_values = (key_own, value_own)
    carried_keys, carried_values = (key_own, value_own)
    moving_keys, moving_values = (key_block, value_block)
    for lag_index in range(1, WIN):
        moving_keys, moving_values = shifted((moving_keys, moving_values), "ctx", 1)
        live_flag = ((position - lag_index >= 0) & (block_mask[0, lag_index - 1] == 1)).astype(
            jnp.float32
        )
        query_term, key_term, value_term = block_terms(moving_keys, moving_values, live_flag)
        grad_query = grad_query + query_term
        carried_keys, carried_values = passed_along((carried_keys, carried_values), "ctx", 1)
        carried_keys = carried_keys + key_term
        carried_values = carried_values + value_term
    home_keys, home_values = (
        passed_along(carried_keys.astype(jnp.bfloat16), "ctx", -(WIN - 1)).astype(
            carried_keys.dtype
        ),
        passed_along(carried_values.astype(jnp.bfloat16), "ctx", -(WIN - 1)).astype(
            carried_values.dtype
        ),
    )
    grad_queries = grad_query.reshape(tokens_here, -1).astype(jnp.bfloat16)
    grad_keys = home_keys.reshape(tokens_here, -1).astype(jnp.bfloat16)
    grad_values = home_values.reshape(tokens_here, -1).astype(jnp.bfloat16)
    experts_here = hidden_saved.shape[0]
    expert_count = experts_here * lax.axis_size("ctx")
    capacity = hidden_saved.shape[1] // lax.axis_size("ctx")
    routed = dispatch_rows(grad_tokens, expert_ids, route_probs, expert_count, capacity)
    received = lax.all_to_all(routed, "ctx", split_axis=0, concat_axis=1, tiled=True)
    grad_weight = jnp.einsum(
        "esf,esd->efd",
        lax.all_gather(hidden_saved, "tp", axis=2, tiled=True),
        received,
        preferred_element_type=jnp.float32,
    ).astype(jnp.bfloat16)
    hidden_sum = lax.psum_scatter(
        jnp.einsum("efd,esd->fes", down_weight, received, preferred_element_type=jnp.float32),
        "tp",
        scatter_dimension=0,
        tiled=True,
    ).transpose(1, 0, 2)
    grad_hidden = hidden_sum.astype(jnp.bfloat16)
    return (grad_queries, grad_keys, grad_values, grad_weight, grad_hidden)


def solution(mesh):
    return jax.shard_map(
        shards,
        mesh=mesh,
        in_specs=(
            P("ctx", "tp"),
            P("ctx", "tp"),
            P("ctx", "tp"),
            P("ctx", "tp"),
            P("ctx", "tp"),
            P("tp", "ctx"),
            P("ctx", None),
            P("ctx", "tp"),
            P("ctx", None),
            P("ctx", None),
            P("ctx", None, "tp"),
            P("ctx", None, "tp"),
        ),
        out_specs=(
            P("ctx", "tp"),
            P("ctx", "tp"),
            P("ctx", "tp"),
            P("ctx", None, "tp"),
            P("ctx", "tp", None),
        ),
        check_vma=False,
    )
```

profile of v0, /device:TPU:25, one launch (start us, length us, event | category | flops | bytes accessed | tf_op | source)
XLA Modules:
  0.0 208.4 jit_solution(8104474181839303750)
XLA Ops:
  7.2 0.8 broadcast_multiply_fusion
  8.0 0.9 copy.102
  8.9 0.1 eq.53
  9.4 0.1 mul.247
  9.5 1.2 reduce-window.6
  10.8 0.2 slice_reduce_fusion
  11.2 2.4 %scatter_custom_fusion = s32[1024]{0:T(1024)S(1)} fusion(s32[512]{0:T(512)S(1)} %bitcast.388, s32[512]{0:T(512)S(1)} %iota_add_fusion, s32[]{:T(128)} %constant.53.clone.1), kind=kCustom, calls=%fused_computation.140 | custom fusion | bytes 4100 | tf_op jit(solution)/shard_map/scatter | solution.py:35
  13.6 0.8 copy.105
  14.6 6.9 %gather_fusion.1 = f32[1024]{0:T(1024)S(1)} fusion(f32[512]{0:T(512)S(1)} %reshape.326, s32[1024]{0:T(1024)S(1)} %get-tuple-element.20), kind=kCustom, calls=%fused_computation.1 | custom fusion | bytes 12288 | tf_op jit(solution)/shard_map/gather | solution.py:38
  21.6 7.1 %gather_fusion = bf16[1024,1024]{1,0:T(8,128)(2,1)} fusion(bf16[256,1024]{1,0:T(8,128)(2,1)} %param.19, s32[1024]{0:T(1024)S(1)} %get-tuple-element.21), kind=kCustom, calls=%fused_computation | custom fusion | bytes 4198400 | tf_op jit(solution)/shard_map/gather | solution.py:39
  28.7 3.3 %fusion = bf16[64,16,1024]{2,1,0:T(8,128)(2,1)} fusion(bf16[64,16,1024]{2,1,0:T(8,128)(2,1)} %bitcast.380, f32[64,16]{1,0:T(8,128)S(1)} %mul.249), kind=kLoop, calls=%fused_computation.5 | loop fusion | flops 3145728 | bytes 4198400 | tf_op jit(solution)/shard_map/convert_element_type | solution.py:40
  32.0 14.0 %all-to-all-start = ((bf16[64,16,1024]{2,1,0:T(8,128)(2,1)}), bf16[64,16,1024]{2,1,0:T(8,128)(2,1)}, u32[]{:S(2)}, u32[]{:S(2)}) async-start(bf16[64,16,1024]{2,1,0:T(8,128)(2,1)} %fusion), calls=%async_computation | async-start | bytes 4194304 | tf_op jit(solution)/shard_map/all_to_all | solution.py:129
  46.1 0.7 all-gather.2.cloned.1.call-update
  46.8 48.9 %all-to-all-done = bf16[64,16,1024]{2,1,0:T(8,128)(2,1)} async-done(((bf16[64,16,1024]{2,1,0:T(8,128)(2,1)}), bf16[64,16,1024]{2,1,0:T(8,128)(2,1)}, u32[]{:S(2)}, u32[]{:S(2)}) %all-to-all-start) | async-done | bytes 2097184 | tf_op jit(solution)/shard_map/all_to_all | solution.py:129
  95.8 7.0 %convolution_bitcast_fusion = f32[1536,1,1024]{0,2,1:T(8,128)} fusion(bf16[1024,1024]{1,0:T(8,128)(2,1)} %bitcast.92, bf16[1,1536,1024]{2,1,0:T(8,128)(2,1)S(1)} %copy-done), kind=kOutput, calls=%fused_computation.3 | convolution fusion | flops 3221225472 | bytes 11534336 | tf_op jit(solution)/shard_map/efd,esd->fes/dot_general | solution.py:137
  102.7 0.8 copy-done.7
  103.6 4.5 %collective-permute-start = (bf16[256,1,128]{2,0,1:T(8,128)(2,1)S(1)}, bf16[256,1,128]{2,0,1:T(8,128)(2,1)S(1)}, u32[]{:S(2)}, u32[]{:S(2)}) collective-permute-start(bf16[256,1,128]{2,0,1:T(8,128)(2,1)S(1)} %bitcast.384), channel_id=1, source_target_pairs={{0,4},{4,8},{8,12},{12,16},{16,20},{20,24},{24,28},{28,32},{32,36}... | collective-permute-start | bytes 196616 | tf_op jit(solution)/shard_map/ppermute | solution.py:13
  108.1 1.9 collective-permute-start.1
  110.0 1.4 multiply_bitcast_fusion
  111.4 1.2 copy.124
  112.6 1.6 reduce_sum.22
  114.3 1.7 fusion.19
  116.0 1.3 fusion.20
  117.3 1.1 fusion.34
  118.4 1.8 collective-permute-start.6
  120.3 1.1 convolution_bitcast_fusion.4
  121.4 2.6 %fusion.91 = f32[8,256,128]{1,2,0:T(8,128)} fusion(bf16[8,256,256]{1,2,0:T(8,128)(2,1)} %copy-done.6, bf16[256,128]{1,0:T(8,128)(2,1)S(1)} %copy-done.7), kind=kOutput, calls=%fused_computation.126 | convolution fusion | flops 134217728 | bytes 2162688 | tf_op jit(solution)/shard_map/kgtu,ukd->tkgd/dot_general | solution.py:88
  123.9 0.6 fusion.99
  126.5 2.2 %collective-permute-start.2 = (bf16[256,1,128]{2,0,1:T(8,128)(2,1)S(1)}, bf16[256,1,128]{2,0,1:T(8,128)(2,1)S(1)}, u32[]{:S(2)}, u32[]{:S(2)}) collective-permute-start(bf16[256,1,128]{2,0,1:T(8,128)(2,1)S(1)} %collective-permute-done), channel_id=1, source_target_pairs={{0,4},{4,8},{8,12},{12,16},{16,20},{20,24},{24,28},{28,32},{32,36}... | collective-permute-start | bytes 196616 | tf_op jit(solution)/shard_map/ppermute | solution.py:13
  128.7 2.3 %collective-permute-start.3 = (bf16[256,1,128]{2,0,1:T(8,128)(2,1)}, bf16[256,1,128]{2,0,1:T(8,128)(2,1)S(1)}, u32[]{:S(2)}, u32[]{:S(2)}) collective-permute-start(bf16[256,1,128]{2,0,1:T(8,128)(2,1)} %collective-permute-done.1), channel_id=1, source_target_pairs={{0,4},{4,8},{8,12},{12,16},{16,20},{20,24},{24,28},{28,32},{32,36}... | collective-permute-start | bytes 196616 | tf_op jit(solution)/shard_map/ppermute | solution.py:13
  131.0 1.6 fusion.15
  132.7 1.4 fusion.21
  134.0 0.4 convolution_add_fusion.2
  134.4 0.7 copy-done.4
  135.1 0.4 fusion.35
  135.6 0.4 fusion.26
  136.0 4.1 %collective-permute-start.11 = (f32[256,1,128]{2,0,1:T(8,128)S(1)}, f32[256,1,128]{2,0,1:T(8,128)S(1)}, u32[]{:S(2)}, u32[]{:S(2)}) collective-permute-start(f32[256,1,128]{2,0,1:T(8,128)S(1)} %fusion.26), channel_id=1, source_target_pairs={{252,0},{0,4},{4,8},{8,12},{12,16},{16,20},{20,24},{24,28},{28,32}... | collective-permute-start | bytes 393224 | tf_op jit(solution)/shard_map/ppermute | solution.py:19
  140.2 4.3 %collective-permute-start.4 = (bf16[256,1,128]{2,0,1:T(8,128)(2,1)S(1)}, bf16[256,1,128]{2,0,1:T(8,128)(2,1)S(1)}, u32[]{:S(2)}, u32[]{:S(2)}) collective-permute-start(bf16[256,1,128]{2,0,1:T(8,128)(2,1)S(1)} %collective-permute-done.2), channel_id=1, source_target_pairs={{0,4},{4,8},{8,12},{12,16},{16,20},{20,24},{24,28},{28,32},{32,36}... | collective-permute-start | bytes 196616 | tf_op jit(solution)/shard_map/ppermute | solution.py:13
  144.4 2.2 %collective-permute-start.5 = (bf16[256,1,128]{2,0,1:T(8,128)(2,1)S(1)}, bf16[256,1,128]{2,0,1:T(8,128)(2,1)S(1)}, u32[]{:S(2)}, u32[]{:S(2)}) collective-permute-start(bf16[256,1,128]{2,0,1:T(8,128)(2,1)S(1)} %collective-permute-done.3), channel_id=1, source_target_pairs={{0,4},{4,8},{8,12},{12,16},{16,20},{20,24},{24,28},{28,32},{32,36}... | collective-permute-start | bytes 196616 | tf_op jit(solution)/shard_map/ppermute | solution.py:13
  146.7 0.6 fusion.11
  147.2 0.4 fusion.22
  147.7 0.4 convolution_bitcast_fusion.2
  148.1 0.4 convolution_add_fusion.1
  148.5 0.4 fusion.30
  148.9 0.6 fusion.7
  149.5 0.4 convolution_bitcast_fusion.1
  149.9 1.6 collective-permute-done.5
  151.6 0.4 fusion.23
  152.1 0.4 fusion.28
  152.6 0.9 collective-permute-start.12
  153.4 5.3 %collective-permute-done.8 = f32[256,1,128]{2,0,1:T(8,128)S(1)} collective-permute-done((f32[256,1,128]{2,0,1:T(8,128)S(1)}, f32[256,1,128]{2,0,1:T(8,128)S(1)}, u32[]{:S(2)}, u32[]{:S(2)}) %collective-permute-start.8) | collective-permute-done | bytes 131104 | tf_op jit(solution)/shard_map/ppermute | solution.py:19
  158.9 1.3 collective-permute-done.12
  160.2 0.3 collective-permute-start.13
  160.5 1.2 fusion.25
  161.7 2.0 copy.106
  163.7 0.5 collective-permute-done.9
  164.2 1.8 collective-permute-done.13
  166.0 7.6 %fusion.1 = bf16[1,1536,1024]{1,2,0:T(8,128)(2,1)} fusion(bf16[1024,1024]{1,0:T(8,128)(2,1)} %bitcast.92, bf16[1,1024,1536]{2,1,0:T(8,128)(2,1)} %all-gather.2.cloned.1.call-done), kind=kOutput, calls=%fused_computation.7 | convolution fusion | flops 3222798336 | bytes 8388608 | tf_op jit(solution)/shard_map/esf,esd->efd/dot_general | solution.py:130
  173.6 4.7 %copy.107 = bf16[1,1536,1024]{2,1,0:T(8,128)(2,1)} copy(bf16[1,1536,1024]{1,2,0:T(8,128)(2,1)} %fusion.1) | data formatting | bytes 6291456
  178.3 17.3 %reduce-scatter.2.cloned.1.call-done = f32[384,1,1024]{0,2,1:T(8,128)} async-done(((f32[1536,1,1024]{0,2,1:T(8,128)}), f32[384,1,1024]{0,2,1:T(8,128)}) %reduce-scatter.2.cloned.1.call-update) | async-done | bytes 1572880 | tf_op jit(solution)/shard_map/reduce_scatter | solution.py:136
  195.6 2.4 %convert_bitcast_fusion = bf16[1,384,1024]{1,2,0:T(8,128)(2,1)} fusion(f32[384,1,1024]{0,2,1:T(8,128)} %reduce-scatter.2.cloned.1.call-done), kind=kLoop, calls=%fused_computation.70 | loop fusion | flops 393216 | bytes 2359296 | tf_op jit(solution)/shard_map/convert_element_type | solution.py:142
  198.0 2.3 %copy.108 = bf16[1,384,1024]{2,1,0:T(8,128)(2,1)} copy(bf16[1,384,1024]{1,2,0:T(8,128)(2,1)} %convert_bitcast_fusion) | data formatting | bytes 1572864
  200.3 0.6 copy.192
  200.9 0.6 copy.193
  (53 shorter events, 1.3 us)
Async XLA Ops:
  7.2 88.6 %copy-start = (bf16[1,1536,1024]{2,1,0:T(8,128)(2,1)S(1)}, bf16[1,1536,1024]{2,1,0:T(8,128)(2,1)}, u32[]{:S(2)}) copy-start(bf16[1,1536,1024]{2,1,0:T(8,128)(2,1)} %param.23) | copy-start | bytes 9437188
  32.0 63.7 %all-to-all-start = ((bf16[64,16,1024]{2,1,0:T(8,128)(2,1)}), bf16[64,16,1024]{2,1,0:T(8,128)(2,1)}, u32[]{:S(2)}, u32[]{:S(2)}) async-start(bf16[64,16,1024]{2,1,0:T(8,128)(2,1)} %fusion), calls=%async_computation | async-start | bytes 4194304 | tf_op jit(solution)/shard_map/all_to_all | solution.py:129
  46.0 119.9 %all-gather.2.cloned.1.call-start = ((), (), s32[]{:S(2)}) async-start(), calls=%async_computation.2 | async-start | bytes 3932160 | tf_op jit(solution)/shard_map/all_gather | solution.py:132
  46.8 148.9 %reduce-scatter.2.cloned.1.call-start = ((), (), s32[]{:S(2)}) async-start(), calls=%async_computation.3 | async-start | bytes 7864320 | tf_op jit(solution)/shard_map/reduce_scatter | solution.py:136
  102.7 0.8 copy-start.7
  103.6 23.0 %collective-permute-start = (bf16[256,1,128]{2,0,1:T(8,128)(2,1)S(1)}, bf16[256,1,128]{2,0,1:T(8,128)(2,1)S(1)}, u32[]{:S(2)}, u32[]{:S(2)}) collective-permute-start(bf16[256,1,128]{2,0,1:T(8,128)(2,1)S(1)} %bitcast.384), channel_id=1, source_target_pairs={{0,4},{4,8},{8,12},{12,16},{16,20},{20,24},{24,28},{28,32},{32,36}... | collective-permute-start | bytes 196616 | tf_op jit(solution)/shard_map/ppermute | solution.py:13
  108.1 20.6 %collective-permute-start.1 = (bf16[256,1,128]{2,0,1:T(8,128)(2,1)}, bf16[256,1,128]{2,0,1:T(8,128)(2,1)}, u32[]{:S(2)}, u32[]{:S(2)}) collective-permute-start(bf16[256,1,128]{2,0,1:T(8,128)(2,1)} %bitcast.17), channel_id=1, source_target_pairs={{0,4},{4,8},{8,12},{12,16},{16,20},{20,24},{24,28},{28,32},{32,36}... | collective-permute-start | bytes 196616 | tf_op jit(solution)/shard_map/ppermute | solution.py:13
  111.4 2.9 %copy-start.8 = (f32[8,256]{1,0:T(8,128)S(1)}, f32[8,256]{1,0:T(8,128)}, u32[]{:S(2)}) copy-start(f32[8,256]{1,0:T(8,128)} %param.17) | copy-start | bytes 24580
  114.2 1.7 copy-start.1
  116.0 1.4 copy-start.3
  117.3 4.0 %copy-start.6 = (bf16[8,256,256]{1,2,0:T(8,128)(2,1)}, bf16[8,256,256]{1,2,0:T(8,128)(2,1)S(1)}, u32[]{:S(2)}) copy-start(bf16[8,256,256]{1,2,0:T(8,128)(2,1)S(1)} %fusion.20) | copy-start | bytes 3145732
  118.4 16.0 %collective-permute-start.6 = (f32[256,1,128]{2,0,1:T(8,128)}, f32[256,1,128]{2,0,1:T(8,128)S(1)}, u32[]{:S(2)}, u32[]{:S(2)}) collective-permute-start(f32[256,1,128]{2,0,1:T(8,128)} %fusion.34), channel_id=1, source_target_pairs={{252,0},{0,4},{4,8},{8,12},{12,16},{16,20},{20,24},{24,28},{28,32}... | collective-permute-start | bytes 393224 | tf_op jit(solution)/shard_map/ppermute | solution.py:19
  121.4 14.2 %collective-permute-start.10 = (f32[256,1,128]{2,0,1:T(8,128)}, f32[256,1,128]{2,0,1:T(8,128)S(1)}, u32[]{:S(2)}, u32[]{:S(2)}) collective-permute-start(f32[256,1,128]{2,0,1:T(8,128)} %convolution_bitcast_fusion.4), channel_id=1, source_target_pairs={{252,0},{0,4},{4,8},{8,12},{12,16},{16,20},{20,24},{24,28},{28,32}... | collective-permute-start | bytes 393224 | tf_op jit(solution)/shard_map/ppermute | solution.py:19
  121.4 2.6 %copy-start.9 = (s32[1,3]{1,0:T(1,128)S(1)}, s32[1,3]{1,0:T(1,128)}, u32[]{:S(2)}) copy-start(s32[1,3]{1,0:T(1,128)} %param.18) | copy-start | bytes 40
  126.5 6.1 %copy-start.2 = (bf16[256,1024]{1,0:T(8,128)(2,1)S(1)}, bf16[256,1024]{1,0:T(8,128)(2,1)}, u32[]{:S(2)}) copy-start(bf16[256,1024]{1,0:T(8,128)(2,1)} %param.16) | copy-start | bytes 1572868
  126.5 13.6 %collective-permute-start.2 = (bf16[256,1,128]{2,0,1:T(8,128)(2,1)S(1)}, bf16[256,1,128]{2,0,1:T(8,128)(2,1)S(1)}, u32[]{:S(2)}, u32[]{:S(2)}) collective-permute-start(bf16[256,1,128]{2,0,1:T(8,128)(2,1)S(1)} %collective-permute-done), channel_id=1, source_target_pairs={{0,4},{4,8},{8,12},{12,16},{16,20},{20,24},{24,28},{28,32},{32,36}... | collective-permute-start | bytes 196616 | tf_op jit(solution)/shard_map/ppermute | solution.py:13
  128.7 15.7 %collective-permute-start.3 = (bf16[256,1,128]{2,0,1:T(8,128)(2,1)}, bf16[256,1,128]{2,0,1:T(8,128)(2,1)S(1)}, u32[]{:S(2)}, u32[]{:S(2)}) collective-permute-start(bf16[256,1,128]{2,0,1:T(8,128)(2,1)} %collective-permute-done.1), channel_id=1, source_target_pairs={{0,4},{4,8},{8,12},{12,16},{16,20},{20,24},{24,28},{28,32},{32,36}... | collective-permute-start | bytes 196616 | tf_op jit(solution)/shard_map/ppermute | solution.py:13
  132.6 1.4 copy-start.5
  134.0 1.0 copy-start.4
  135.5 16.5 %collective-permute-start.7 = (f32[256,1,128]{2,0,1:T(8,128)S(1)}, f32[256,1,128]{2,0,1:T(8,128)S(1)}, u32[]{:S(2)}, u32[]{:S(2)}) collective-permute-start(f32[256,1,128]{2,0,1:T(8,128)S(1)} %fusion.35), channel_id=1, source_target_pairs={{252,0},{0,4},{4,8},{8,12},{12,16},{16,20},{20,24},{24,28},{28,32}... | collective-permute-start | bytes 393224 | tf_op jit(solution)/shard_map/ppermute | solution.py:19
  136.0 16.5 %collective-permute-start.11 = (f32[256,1,128]{2,0,1:T(8,128)S(1)}, f32[256,1,128]{2,0,1:T(8,128)S(1)}, u32[]{:S(2)}, u32[]{:S(2)}) collective-permute-start(f32[256,1,128]{2,0,1:T(8,128)S(1)} %fusion.26), channel_id=1, source_target_pairs={{252,0},{0,4},{4,8},{8,12},{12,16},{16,20},{20,24},{24,28},{28,32}... | collective-permute-start | bytes 393224 | tf_op jit(solution)/shard_map/ppermute | solution.py:19
  140.2 8.8 %collective-permute-start.4 = (bf16[256,1,128]{2,0,1:T(8,128)(2,1)S(1)}, bf16[256,1,128]{2,0,1:T(8,128)(2,1)S(1)}, u32[]{:S(2)}, u32[]{:S(2)}) collective-permute-start(bf16[256,1,128]{2,0,1:T(8,128)(2,1)S(1)} %collective-permute-done.2), channel_id=1, source_target_pairs={{0,4},{4,8},{8,12},{12,16},{16,20},{20,24},{24,28},{28,32},{32,36}... | collective-permute-start | bytes 196616 | tf_op jit(solution)/shard_map/ppermute | solution.py:13
  144.4 7.1 %collective-permute-start.5 = (bf16[256,1,128]{2,0,1:T(8,128)(2,1)S(1)}, bf16[256,1,128]{2,0,1:T(8,128)(2,1)S(1)}, u32[]{:S(2)}, u32[]{:S(2)}) collective-permute-start(bf16[256,1,128]{2,0,1:T(8,128)(2,1)S(1)} %collective-permute-done.3), channel_id=1, source_target_pairs={{0,4},{4,8},{8,12},{12,16},{16,20},{20,24},{24,28},{28,32},{32,36}... | collective-permute-start | bytes 196616 | tf_op jit(solution)/shard_map/ppermute | solution.py:13
  152.0 6.7 %collective-permute-start.8 = (f32[256,1,128]{2,0,1:T(8,128)S(1)}, f32[256,1,128]{2,0,1:T(8,128)S(1)}, u32[]{:S(2)}, u32[]{:S(2)}) collective-permute-start(f32[256,1,128]{2,0,1:T(8,128)S(1)} %add.90), channel_id=1, source_target_pairs={{252,0},{0,4},{4,8},{8,12},{12,16},{16,20},{20,24},{24,28},{28,32}... | collective-permute-start | bytes 393224 | tf_op jit(solution)/shard_map/ppermute | solution.py:19
  152.6 7.6 %collective-permute-start.12 = (f32[256,1,128]{2,0,1:T(8,128)S(1)}, f32[256,1,128]{2,0,1:T(8,128)S(1)}, u32[]{:S(2)}, u32[]{:S(2)}) collective-permute-start(f32[256,1,128]{2,0,1:T(8,128)S(1)} %add.93), channel_id=1, source_target_pairs={{252,0},{0,4},{4,8},{8,12},{12,16},{16,20},{20,24},{24,28},{28,32}... | collective-permute-start | bytes 393224 | tf_op jit(solution)/shard_map/ppermute | solution.py:19
  158.8 5.4 %collective-permute-start.9 = (bf16[256,1,128]{2,0,1:T(8,128)(2,1)S(1)}, bf16[256,1,128]{2,0,1:T(8,128)(2,1)S(1)}, u32[]{:S(2)}, u32[]{:S(2)}) collective-permute-start(bf16[256,1,128]{2,0,1:T(8,128)(2,1)S(1)} %add_convert_fusion.1), channel_id=1, source_target_pairs={{12,0},{16,4},{20,8},{24,12},{28,16},{32,20},{36,24},{40,28},{44,3... | collective-permute-start | bytes 196616 | tf_op jit(solution)/shard_map/ppermute | solution.py:19
  160.2 5.8 %collective-permute-start.13 = (bf16[256,1,128]{2,0,1:T(8,128)(2,1)S(1)}, bf16[256,1,128]{2,0,1:T(8,128)(2,1)S(1)}, u32[]{:S(2)}, u32[]{:S(2)}) collective-permute-start(bf16[256,1,128]{2,0,1:T(8,128)(2,1)S(1)} %add_convert_fusion), channel_id=1, source_target_pairs={{12,0},{16,4},{20,8},{24,12},{28,16},{32,20},{36,24},{40,28},{44,3... | collective-permute-start | bytes 196616 | tf_op jit(solution)/shard_map/ppermute | solution.py:19
Sparse Core Ops, SparseCore 0:
  48.7 56.5 all-gather.1
  107.9 87.6 reduce-scatter.1
where the time goes:
time: 209 us; the launch traced here: 208 us
  waiting for transfers between devices  77.5 us (37%)
  starting transfers between devices  38.9 us (19%)
  local copies, waits for them, and re-layouts  32.8 us (16%)
  matrix products  31.8 us (15%)
  between operations  16.5 us (8%)
  other arithmetic  11 us (5%)
    all_to_all x1, waiting for transfers between devices, shards(): lax.all_to_all(routed, 'ctx', split_axis=0, concat_axis=1, tiled=True)  48.9 us
    ppermute x6, starting transfers between devices, shifted(): return lax.ppermute(x, axis, pairs)  17.4 us
    reduce_scatter x1, waiting for transfers between devices, shards(): lax.psum_scatter(jnp.einsum('efd,esd->fes', down_weight, received, prefer...  17.3 us
    unnamed x28, local copies, waits for them, and re-layouts  14.7 us
    all_to_all x1, starting transfers between devices, shards(): lax.all_to_all(routed, 'ctx', split_axis=0, concat_axis=1, tiled=True)  14 us
    ppermute x8, waiting for transfers between devices, passed_along(): return lax.ppermute(block, axis, route)  8.85 us
    dot_general x1, matrix products, shards(): jnp.einsum('esf,esd->efd', lax.all_gather(hidden_saved, 'tp', axis=2, til...  7.65 us
    ppermute x8, starting transfers between devices, passed_along(): return lax.ppermute(block, axis, route)  7.41 us
  transfers between devices with their start and end apart: 17, of which 7 were waited for; matrix products, arithmetic and copies ran while one was open for 21% of the time, Pallas kernels for 0%

commit v1 on v0

--- a/solution.py
+++ b/solution.py
@@ -1,10 +1,15 @@
 import jax
 import jax.numpy as jnp
 from jax import lax
+from jax.experimental import pallas as pl
+from jax.experimental.pallas import tpu as pltpu
 from jax.sharding import PartitionSpec as P
 
 HD = 128
 WIN = 4
+CTX = 64
+CAP = 16
+MESH = pl.DeviceIdType.MESH
 
 
 def shifted(x, axis, by):
@@ -19,25 +24,93 @@
     return lax.ppermute(block, axis, route)
 
 
-def dispatch_rows(grad_rows, expert_ids, route_probs, expert_count, capacity):
-    top_count = expert_ids.shape[1]
-    route_count = expert_ids.shape[0] * top_count
-    flat_ids = expert_ids.reshape(-1)
-    one_hot = (flat_ids[:, None] == jnp.arange(expert_count, dtype=jnp.int32)[None, :]).astype(
-        jnp.int32
-    )
-    earlier = jnp.cumsum(one_hot, axis=0, dtype=jnp.int32) - one_hot
-    slot_index = jnp.sum(earlier * one_hot, axis=1, dtype=jnp.int32)
-    target = flat_ids * capacity + slot_index
-    source = (
-        jnp.zeros((expert_count * capacity,), jnp.int32)
-        .at[target]
-        .set(jnp.arange(route_count, dtype=jnp.int32) + 1)
-    )
-    chosen = jnp.maximum(source - 1, 0)
-    factor = jnp.where(source > 0, route_probs.reshape(-1)[chosen], 0.0)
-    picked = grad_rows[chosen // top_count].astype(jnp.float32) * factor[:, None]
-    return picked.astype(jnp.bfloat16).reshape(expert_count, capacity, grad_rows.shape[1])
+def place(ctx, offset):
+    x = lax.rem(ctx // 32 + offset // 32, 2)
+    y = lax.rem(lax.rem(ctx // 8, 4) + lax.rem(offset // 8, 4), 4)
+    z = lax.rem(lax.rem(ctx, 8) + lax.rem(offset, 8), 8)
+    return (x * 4 + y) * 8 + z
+
+
+def exchange_kernel(tokens, ids, probs, received, routed, chosen, send_sem, recv_sems):
+    ctx, tp = lax.axis_index("ctx"), lax.axis_index("tp")
+    barrier = pltpu.get_barrier_semaphore()
+
+    def greet(offset, carry):
+        pl.semaphore_signal(barrier, inc=1, device_id=(place(ctx, offset), tp), device_id_type=MESH)
+        return carry
+
+    lax.fori_loop(1, CTX, greet, 0)
+
+    count = tokens.shape[0]
+    lanes = lax.broadcasted_iota(jnp.int32, (count, 128), 1)
+    first, second = ids[:, 0:1] == lanes, ids[:, 1:2] == lanes
+    both = (first | second).astype(jnp.bfloat16)
+    below = (
+        lax.broadcasted_iota(jnp.int32, (count, count), 0)
+        > lax.broadcasted_iota(jnp.int32, (count, count), 1)
+    ).astype(jnp.bfloat16)
+    earlier = jnp.dot(below, both, preferred_element_type=jnp.float32)
+    slots = []
+    for rank, one_hot in enumerate((first, second)):
+        slot = jnp.sum(jnp.where(one_hot, earlier, 0.0), axis=1, keepdims=True).astype(jnp.int32)
+        slots.append(ids[:, rank : rank + 1] * CAP + slot)
+        chosen[pl.ds(rank * count, count), :] = (
+            tokens[...].astype(jnp.float32) * probs[:, rank : rank + 1]
+        ).astype(jnp.bfloat16)
+
+    def pick(column, carry):
+        wanted = lanes + column * 128
+        select = jnp.concatenate(
+            [(slot == wanted).astype(jnp.bfloat16) for slot in slots], axis=0
+        )
+        routed[pl.ds(column * 128, 128), :] = lax.dot_general(
+            select, chosen[...], (((0,), (0,)), ((), ())), preferred_element_type=jnp.float32
+        ).astype(jnp.bfloat16)
+        return carry
+
+    lax.fori_loop(0, 8, pick, 0)
+    pl.semaphore_wait(barrier, CTX - 1)
+
+    def send(offset, carry):
+        target = place(ctx, offset)
+        pltpu.make_async_remote_copy(
+            src_ref=routed.at[pl.ds(target * CAP, CAP)],
+            dst_ref=received.at[pl.ds(ctx * CAP, CAP)],
+            send_sem=send_sem,
+            recv_sem=recv_sems.at[offset // 8],
+            device_id=(target, tp),
+            device_id_type=MESH,
+        ).start()
+        return carry
+
+    lax.fori_loop(1, CTX, send, 0)
+    received[pl.ds(ctx * CAP, CAP), :] = routed[pl.ds(ctx * CAP, CAP), :]
+    for column in range(8):
+        rows = pl.ds(0, 112 if column == 0 else 128)
+        pltpu.make_async_copy(received.at[rows], received.at[rows], recv_sems.at[column]).wait()
+    rows = pl.ds(0, (CTX - 1) * CAP)
+    pltpu.make_async_copy(routed.at[rows], routed.at[rows], send_sem).wait()
+
+
+def exchanged(tokens, ids, probs):
+    width = tokens.shape[1]
+    vmem = pl.BlockSpec(memory_space=pltpu.VMEM)
+    return pl.pallas_call(
+        exchange_kernel,
+        out_shape=jax.ShapeDtypeStruct((CTX * CAP, width), jnp.bfloat16),
+        in_specs=[vmem] * 3,
+        out_specs=vmem,
+        scratch_shapes=[
+            pltpu.VMEM((CTX * CAP, width), jnp.bfloat16),
+            pltpu.VMEM((2 * tokens.shape[0], width), jnp.bfloat16),
+            pltpu.SemaphoreType.DMA,
+            pltpu.SemaphoreType.DMA((8,)),
+        ],
+        compiler_params=pltpu.CompilerParams(
+            collective_id=0, has_side_effects=True, vmem_limit_bytes=32 * 2**20
+        ),
+        name="exchange",
+    )(tokens, ids, probs)
 
 
 def shards(
@@ -122,11 +195,7 @@
     grad_queries = grad_query.reshape(tokens_here, -1).astype(jnp.bfloat16)
     grad_keys = home_keys.reshape(tokens_here, -1).astype(jnp.bfloat16)
     grad_values = home_values.reshape(tokens_here, -1).astype(jnp.bfloat16)
-    experts_here = hidden_saved.shape[0]
-    expert_count = experts_here * lax.axis_size("ctx")
-    capacity = hidden_saved.shape[1] // lax.axis_size("ctx")
-    routed = dispatch_rows(grad_tokens, expert_ids, route_probs, expert_count, capacity)
-    received = lax.all_to_all(routed, "ctx", split_axis=0, concat_axis=1, tiled=True)
+    received = exchanged(grad_tokens, expert_ids, route_probs)[None]
     grad_weight = jnp.einsum(
         "esf,esd->efd",
         lax.all_gather(hidden_saved, "tp", axis=2, tiled=True),

time: 209 us -> 180 us (0.86)
  Pallas kernels: 0 us -> 59 us
  waiting for transfers between devices: 77.5 us -> 23.8 us
  local copies, waits for them, and re-layouts: 32.8 us -> 17.8 us
  starting transfers between devices: 38.9 us -> 26.4 us
  other arithmetic: 11 us -> 5.41 us
    pallas_call x0 -> x1, Pallas kernels: none -> 59 us  [exchanged(): pl.pallas_call(exchange_kernel, out_shape=jax.ShapeDtypeStruct((CTX * CAP...]
    all_to_all x1 -> x0, waiting for transfers between devices: 48.9 us -> none  [shards(): lax.all_to_all(routed, 'ctx', split_axis=0, concat_axis=1, tiled=True)]
    all_to_all x1 -> x0, starting transfers between devices: 14 us -> none  [shards(): lax.all_to_all(routed, 'ctx', split_axis=0, concat_axis=1, tiled=True)]
    gather x2 -> x0, local copies, waits for them, and re-layouts: 14 us -> none  [the longest x1 7.12 us: dispatch_rows(): grad_rows[chosen // top_count].astype(jnp.float32) * factor[:, None]]
    convert_element_type x2 -> x0, other arithmetic: 3.33 us -> none  [the longest x1 3.32 us: dispatch_rows(): picked.astype(jnp.bfloat16)]
    scatter x1 -> x0, local copies, waits for them, and re-layouts: 2.45 us -> none  [dispatch_rows(): source = jnp.zeros((expert_count * capacity,), jnp.int32).at[target].set(...]
    unnamed x28 -> x32, local copies, waits for them, and re-layouts: 14.7 us -> 17.1 us
    ppermute x8, starting transfers between devices: 7.41 us -> 9.82 us  [passed_along(): return lax.ppermute(block, axis, route)]
  transfers between devices with their start and end apart: 17 -> 16, of which waited for: 7 -> 6; matrix products, arithmetic and copies ran while one was open for 21% -> 24% of each run, Pallas kernels for 0% -> 33%
where the time goes in v1:
time: 180 us; the launch traced here: 179 us
  Pallas kernels  59 us (33%)
  matrix products  30.4 us (17%)
  starting transfers between devices  26.4 us (15%)
  waiting for transfers between devices  23.8 us (13%)
  local copies, waits for them, and re-layouts  17.8 us (10%)
  between operations  16.5 us (9%)
  other arithmetic  5.41 us (3%)
    pallas_call x1, Pallas kernels, exchanged(): pl.pallas_call(exchange_kernel, out_shape=jax.ShapeDtypeStruct((CTX * CAP...  59 us
    unnamed x32, local copies, waits for them, and re-layouts  17.1 us
    ppermute x6, starting transfers between devices, shifted(): return lax.ppermute(x, axis, pairs)  16.5 us
    reduce_scatter x1, waiting for transfers between devices, shards(): lax.psum_scatter(jnp.einsum('efd,esd->fes', down_weight, received, prefer...  15.7 us
    ppermute x8, starting transfers between devices, passed_along(): return lax.ppermute(block, axis, route)  9.82 us
    dot_general x1, matrix products, shards(): jnp.einsum('esf,esd->efd', lax.all_gather(hidden_saved, 'tp', axis=2, til...  7.66 us
    ppermute x8, waiting for transfers between devices, passed_along(): return lax.ppermute(block, axis, route)  6.74 us
    dot_general x1, matrix products, shards(): jnp.einsum('efd,esd->fes', down_weight, received, preferred_element_type=...  5.49 us
  transfers between devices with their start and end apart: 16, of which 6 were waited for; matrix products, arithmetic and copies ran while one was open for 24% of the time, Pallas kernels for 33%

profile of v1, /device:TPU:25, one launch (start us, length us, event | category | flops | bytes accessed | tf_op | source)
XLA Modules:
  0.0 179.3 jit_solution(3618083042273014961)
XLA Ops:
  7.2 0.0 copy-start
  7.2 0.0 all-gather.2.cloned.1.call-start
  7.2 0.7 all-gather.2.cloned.1.call-update
  7.9 0.0 reduce-scatter.2.cloned.1.call-start
  8.0 1.0 copy.71.ids
  8.9 0.8 copy.72.probs
  9.8 1.0 copy-done.2
  10.8 59.0 %exchange.1 = bf16[1024,1024]{1,0:T(8,128)(2,1)S(1)} custom-call(bf16[256,1024]{1,0:T(8,128)(2,1)S(1)} %copy-done.2, s32[256,2]{1,0:T(8,128)S(1)} %copy.71.ids, f32[256,2]{1,0:T(8,128)S(1)} %copy.72.probs), custom_call_target="tpu_custom_call" | custom-call | tf_op jit(solution)/shard_map/exchange/pallas_call | solution.py:98
  69.8 1.3 copy-done.1
  71.2 5.5 %convolution_bitcast_fusion = f32[1536,1,1024]{0,2,1:T(8,128)} fusion(bf16[1024,1024]{1,0:T(8,128)(2,1)S(1)} %exchange.1, bf16[1,1536,1024]{2,1,0:T(8,128)(2,1)S(1)} %copy-done), kind=kOutput, calls=%fused_computation | convolution fusion | flops 3221225472 | bytes 11534336 | tf_op jit(solution)/shard_map/efd,esd->fes/dot_general | solution.py:206
  76.6 0.0 reduce-scatter.2.cloned.1.call-update
  76.7 0.8 copy-done.9
  77.5 2.8 %collective-permute-start = (bf16[256,1,128]{2,0,1:T(8,128)(2,1)S(1)}, bf16[256,1,128]{2,0,1:T(8,128)(2,1)S(1)}, u32[]{:S(2)}, u32[]{:S(2)}) collective-permute-start(bf16[256,1,128]{2,0,1:T(8,128)(2,1)S(1)} %bitcast.358), channel_id=1, source_target_pairs={{0,4},{4,8},{8,12},{12,16},{16,20},{20,24},{24,28},{28,32},{32,36}... | collective-permute-start | bytes 196616 | tf_op jit(solution)/shard_map/ppermute | solution.py:18
  80.3 3.1 %collective-permute-start.1 = (bf16[256,1,128]{2,0,1:T(8,128)(2,1)}, bf16[256,1,128]{2,0,1:T(8,128)(2,1)}, u32[]{:S(2)}, u32[]{:S(2)}) collective-permute-start(bf16[256,1,128]{2,0,1:T(8,128)(2,1)} %bitcast.17), channel_id=1, source_target_pairs={{0,4},{4,8},{8,12},{12,16},{16,20},{20,24},{24,28},{28,32},{32,36}... | collective-permute-start | bytes 196616 | tf_op jit(solution)/shard_map/ppermute | solution.py:18
  83.4 1.4 multiply_bitcast_fusion
  84.8 1.2 copy.90
  86.0 1.6 reduce_sum.11
  87.6 0.1 copy.48
  87.7 1.7 fusion.18
  89.4 1.4 fusion.19
  90.8 1.1 fusion.33
  91.8 1.1 convolution_bitcast_fusion.4
  92.9 2.6 %collective-permute-start.10 = (f32[256,1,128]{2,0,1:T(8,128)}, f32[256,1,128]{2,0,1:T(8,128)S(1)}, u32[]{:S(2)}, u32[]{:S(2)}) collective-permute-start(f32[256,1,128]{2,0,1:T(8,128)} %convolution_bitcast_fusion.4), channel_id=1, source_target_pairs={{252,0},{0,4},{4,8},{8,12},{12,16},{16,20},{20,24},{24,28},{28,32}... | collective-permute-start | bytes 393224 | tf_op jit(solution)/shard_map/ppermute | solution.py:24
  95.6 2.6 %fusion.86 = f32[8,256,128]{1,2,0:T(8,128)} fusion(bf16[8,256,256]{1,2,0:T(8,128)(2,1)} %copy-done.8, bf16[256,128]{1,0:T(8,128)(2,1)S(1)} %copy-done.9), kind=kOutput, calls=%fused_computation.112 | convolution fusion | flops 134217728 | bytes 2162688 | tf_op jit(solution)/shard_map/kgtu,ukd->tkgd/dot_general | solution.py:161
  98.2 0.7 fusion.89
  100.9 2.1 %collective-permute-start.2 = (bf16[256,1,128]{2,0,1:T(8,128)(2,1)S(1)}, bf16[256,1,128]{2,0,1:T(8,128)(2,1)S(1)}, u32[]{:S(2)}, u32[]{:S(2)}) collective-permute-start(bf16[256,1,128]{2,0,1:T(8,128)(2,1)S(1)} %collective-permute-done), channel_id=1, source_target_pairs={{0,4},{4,8},{8,12},{12,16},{16,20},{20,24},{24,28},{28,32},{32,36}... | collective-permute-start | bytes 196616 | tf_op jit(solution)/shard_map/ppermute | solution.py:18
  102.9 2.4 %collective-permute-start.3 = (bf16[256,1,128]{2,0,1:T(8,128)(2,1)}, bf16[256,1,128]{2,0,1:T(8,128)(2,1)S(1)}, u32[]{:S(2)}, u32[]{:S(2)}) collective-permute-start(bf16[256,1,128]{2,0,1:T(8,128)(2,1)} %collective-permute-done.1), channel_id=1, source_target_pairs={{0,4},{4,8},{8,12},{12,16},{16,20},{20,24},{24,28},{28,32},{32,36}... | collective-permute-start | bytes 196616 | tf_op jit(solution)/shard_map/ppermute | solution.py:18
  105.4 1.6 fusion.14
  107.0 1.4 fusion.20
  108.4 0.4 convolution_add_fusion.2
  108.8 0.7 copy-done.6
  109.4 0.4 fusion.34
  109.9 1.1 collective-permute-start.7
  111.0 0.4 fusion.25
  111.4 3.3 %collective-permute-start.11 = (f32[256,1,128]{2,0,1:T(8,128)S(1)}, f32[256,1,128]{2,0,1:T(8,128)S(1)}, u32[]{:S(2)}, u32[]{:S(2)}) collective-permute-start(f32[256,1,128]{2,0,1:T(8,128)S(1)} %fusion.25), channel_id=1, source_target_pairs={{252,0},{0,4},{4,8},{8,12},{12,16},{16,20},{20,24},{24,28},{28,32}... | collective-permute-start | bytes 393224 | tf_op jit(solution)/shard_map/ppermute | solution.py:24
  114.8 2.9 %collective-permute-start.4 = (bf16[256,1,128]{2,0,1:T(8,128)(2,1)S(1)}, bf16[256,1,128]{2,0,1:T(8,128)(2,1)S(1)}, u32[]{:S(2)}, u32[]{:S(2)}) collective-permute-start(bf16[256,1,128]{2,0,1:T(8,128)(2,1)S(1)} %collective-permute-done.2), channel_id=1, source_target_pairs={{0,4},{4,8},{8,12},{12,16},{16,20},{20,24},{24,28},{28,32},{32,36}... | collective-permute-start | bytes 196616 | tf_op jit(solution)/shard_map/ppermute | solution.py:18
  117.7 3.2 %collective-permute-start.5 = (bf16[256,1,128]{2,0,1:T(8,128)(2,1)S(1)}, bf16[256,1,128]{2,0,1:T(8,128)(2,1)S(1)}, u32[]{:S(2)}, u32[]{:S(2)}) collective-permute-start(bf16[256,1,128]{2,0,1:T(8,128)(2,1)S(1)} %collective-permute-done.3), channel_id=1, source_target_pairs={{0,4},{4,8},{8,12},{12,16},{16,20},{20,24},{24,28},{28,32},{32,36}... | collective-permute-start | bytes 196616 | tf_op jit(solution)/shard_map/ppermute | solution.py:18
  120.9 0.6 fusion.10
  121.5 0.4 fusion.21
  121.9 0.4 convolution_bitcast_fusion.2
  122.4 0.4 convolution_add_fusion.1
  122.7 0.4 fusion.29
  123.2 0.6 fusion.6
  123.7 0.4 convolution_bitcast_fusion.1
  124.2 0.6 collective-permute-done.5
  124.8 0.4 fusion.22
  125.3 0.1 collective-permute-start.8
  125.4 0.4 fusion.27
  125.8 1.8 %collective-permute-start.12 = (f32[256,1,128]{2,0,1:T(8,128)S(1)}, f32[256,1,128]{2,0,1:T(8,128)S(1)}, u32[]{:S(2)}, u32[]{:S(2)}) collective-permute-start(f32[256,1,128]{2,0,1:T(8,128)S(1)} %add.54), channel_id=1, source_target_pairs={{252,0},{0,4},{4,8},{8,12},{12,16},{16,20},{20,24},{24,28},{28,32}... | collective-permute-start | bytes 393224 | tf_op jit(solution)/shard_map/ppermute | solution.py:24
  127.6 3.6 %collective-permute-done.8 = f32[256,1,128]{2,0,1:T(8,128)S(1)} collective-permute-done((f32[256,1,128]{2,0,1:T(8,128)S(1)}, f32[256,1,128]{2,0,1:T(8,128)S(1)}, u32[]{:S(2)}, u32[]{:S(2)}) %collective-permute-start.8) | collective-permute-done | bytes 131104 | tf_op jit(solution)/shard_map/ppermute | solution.py:24
  131.3 0.1 collective-permute-start.9
  131.4 1.3 collective-permute-done.12
  132.7 0.7 collective-permute-start.13
  133.4 1.2 fusion.24
  134.6 2.0 %copy.73 = bf16[256,1024]{1,0:T(8,128)(2,1)} copy(bf16[256,1024]{0,1:T(8,128)(2,1)} %bitcast.356) | data formatting | bytes 1048576
  136.7 1.0 collective-permute-done.9
  137.7 0.8 collective-permute-done.13
  138.5 7.7 %fusion = bf16[1,1536,1024]{1,2,0:T(8,128)(2,1)} fusion(bf16[1024,1024]{1,0:T(8,128)(2,1)} %copy-done.1, bf16[1,1024,1536]{2,1,0:T(8,128)(2,1)} %all-gather.2.cloned.1.call-done), kind=kOutput, calls=%fused_computation.2 | convolution fusion | flops 3222798336 | bytes 8388608 | tf_op jit(solution)/shard_map/esf,esd->efd/dot_general | solution.py:199
  146.1 4.7 %copy.74 = bf16[1,1536,1024]{2,1,0:T(8,128)(2,1)} copy(bf16[1,1536,1024]{1,2,0:T(8,128)(2,1)} %fusion) | data formatting | bytes 6291456
  150.8 15.7 %reduce-scatter.2.cloned.1.call-done = f32[384,1,1024]{0,2,1:T(8,128)} async-done(((f32[1536,1,1024]{0,2,1:T(8,128)}), f32[384,1,1024]{0,2,1:T(8,128)}) %reduce-scatter.2.cloned.1.call-update) | async-done | bytes 1572880 | tf_op jit(solution)/shard_map/reduce_scatter | solution.py:205
  166.5 2.4 %convert_bitcast_fusion = bf16[1,384,1024]{1,2,0:T(8,128)(2,1)} fusion(f32[384,1,1024]{0,2,1:T(8,128)} %reduce-scatter.2.cloned.1.call-done), kind=kLoop, calls=%fused_computation.65 | loop fusion | flops 393216 | bytes 2359296 | tf_op jit(solution)/shard_map/convert_element_type | solution.py:211
  168.9 2.3 %copy.75 = bf16[1,384,1024]{2,1,0:T(8,128)(2,1)} copy(bf16[1,384,1024]{1,2,0:T(8,128)(2,1)} %convert_bitcast_fusion) | data formatting | bytes 1572864
  171.2 0.6 copy.157
  171.8 0.6 copy.158
  (35 shorter events, 0.2 us)
Async XLA Ops:
  7.2 64.0 %copy-start = (bf16[1,1536,1024]{2,1,0:T(8,128)(2,1)S(1)}, bf16[1,1536,1024]{2,1,0:T(8,128)(2,1)}, u32[]{:S(2)}) copy-start(bf16[1,1536,1024]{2,1,0:T(8,128)(2,1)} %param.23) | copy-start | bytes 9437188
  7.2 131.3 %all-gather.2.cloned.1.call-start = ((), (), s32[]{:S(2)}) async-start(), calls=%async_computation.1 | async-start | bytes 3932160 | tf_op jit(solution)/shard_map/all_gather | solution.py:201
  7.9 158.6 %reduce-scatter.2.cloned.1.call-start = ((), (), s32[]{:S(2)}) async-start(), calls=%async_computation.2 | async-start | bytes 7864320 | tf_op jit(solution)/shard_map/reduce_scatter | solution.py:205
  9.8 1.0 copy-start.2
  69.8 1.3 copy-start.1
  76.6 0.8 copy-start.9
  77.5 23.4 %collective-permute-start = (bf16[256,1,128]{2,0,1:T(8,128)(2,1)S(1)}, bf16[256,1,128]{2,0,1:T(8,128)(2,1)S(1)}, u32[]{:S(2)}, u32[]{:S(2)}) collective-permute-start(bf16[256,1,128]{2,0,1:T(8,128)(2,1)S(1)} %bitcast.358), channel_id=1, source_target_pairs={{0,4},{4,8},{8,12},{12,16},{16,20},{20,24},{24,28},{28,32},{32,36}... | collective-permute-start | bytes 196616 | tf_op jit(solution)/shard_map/ppermute | solution.py:18
  80.3 22.6 %collective-permute-start.1 = (bf16[256,1,128]{2,0,1:T(8,128)(2,1)}, bf16[256,1,128]{2,0,1:T(8,128)(2,1)}, u32[]{:S(2)}, u32[]{:S(2)}) collective-permute-start(bf16[256,1,128]{2,0,1:T(8,128)(2,1)} %bitcast.17), channel_id=1, source_target_pairs={{0,4},{4,8},{8,12},{12,16},{16,20},{20,24},{24,28},{28,32},{32,36}... | collective-permute-start | bytes 196616 | tf_op jit(solution)/shard_map/ppermute | solution.py:18
  84.8 2.9 %copy-start.10 = (f32[8,256]{1,0:T(8,128)S(1)}, f32[8,256]{1,0:T(8,128)}, u32[]{:S(2)}) copy-start(f32[8,256]{1,0:T(8,128)} %param.17) | copy-start | bytes 24580
  87.6 1.7 copy-start.3
  89.4 1.4 copy-start.5
  90.7 2.2 %copy-start.8 = (bf16[8,256,256]{1,2,0:T(8,128)(2,1)}, bf16[8,256,256]{1,2,0:T(8,128)(2,1)S(1)}, u32[]{:S(2)}) copy-start(bf16[8,256,256]{1,2,0:T(8,128)(2,1)S(1)} %fusion.19) | copy-start | bytes 3145732
  91.8 16.9 %collective-permute-start.6 = (f32[256,1,128]{2,0,1:T(8,128)}, f32[256,1,128]{2,0,1:T(8,128)S(1)}, u32[]{:S(2)}, u32[]{:S(2)}) collective-permute-start(f32[256,1,128]{2,0,1:T(8,128)} %fusion.33), channel_id=1, source_target_pairs={{252,0},{0,4},{4,8},{8,12},{12,16},{16,20},{20,24},{24,28},{28,32}... | collective-permute-start | bytes 393224 | tf_op jit(solution)/shard_map/ppermute | solution.py:24
  92.9 18.1 %collective-permute-start.10 = (f32[256,1,128]{2,0,1:T(8,128)}, f32[256,1,128]{2,0,1:T(8,128)S(1)}, u32[]{:S(2)}, u32[]{:S(2)}) collective-permute-start(f32[256,1,128]{2,0,1:T(8,128)} %convolution_bitcast_fusion.4), channel_id=1, source_target_pairs={{252,0},{0,4},{4,8},{8,12},{12,16},{16,20},{20,24},{24,28},{28,32}... | collective-permute-start | bytes 393224 | tf_op jit(solution)/shard_map/ppermute | solution.py:24
  95.6 2.6 %copy-start.11 = (s32[1,3]{1,0:T(1,128)S(1)}, s32[1,3]{1,0:T(1,128)}, u32[]{:S(2)}) copy-start(s32[1,3]{1,0:T(1,128)} %param.18) | copy-start | bytes 40
  100.8 6.2 %copy-start.4 = (bf16[256,1024]{1,0:T(8,128)(2,1)S(1)}, bf16[256,1024]{1,0:T(8,128)(2,1)}, u32[]{:S(2)}) copy-start(bf16[256,1024]{1,0:T(8,128)(2,1)} %param.16) | copy-start | bytes 1572868
  100.9 13.9 %collective-permute-start.2 = (bf16[256,1,128]{2,0,1:T(8,128)(2,1)S(1)}, bf16[256,1,128]{2,0,1:T(8,128)(2,1)S(1)}, u32[]{:S(2)}, u32[]{:S(2)}) collective-permute-start(bf16[256,1,128]{2,0,1:T(8,128)(2,1)S(1)} %collective-permute-done), channel_id=1, source_target_pairs={{0,4},{4,8},{8,12},{12,16},{16,20},{20,24},{24,28},{28,32},{32,36}... | collective-permute-start | bytes 196616 | tf_op jit(solution)/shard_map/ppermute | solution.py:18
  102.9 14.7 %collective-permute-start.3 = (bf16[256,1,128]{2,0,1:T(8,128)(2,1)}, bf16[256,1,128]{2,0,1:T(8,128)(2,1)S(1)}, u32[]{:S(2)}, u32[]{:S(2)}) collective-permute-start(bf16[256,1,128]{2,0,1:T(8,128)(2,1)} %collective-permute-done.1), channel_id=1, source_target_pairs={{0,4},{4,8},{8,12},{12,16},{16,20},{20,24},{24,28},{28,32},{32,36}... | collective-permute-start | bytes 196616 | tf_op jit(solution)/shard_map/ppermute | solution.py:18
  107.0 1.4 copy-start.7
  108.4 1.0 copy-start.6
  109.9 15.4 %collective-permute-start.7 = (f32[256,1,128]{2,0,1:T(8,128)S(1)}, f32[256,1,128]{2,0,1:T(8,128)S(1)}, u32[]{:S(2)}, u32[]{:S(2)}) collective-permute-start(f32[256,1,128]{2,0,1:T(8,128)S(1)} %fusion.34), channel_id=1, source_target_pairs={{252,0},{0,4},{4,8},{8,12},{12,16},{16,20},{20,24},{24,28},{28,32}... | collective-permute-start | bytes 393224 | tf_op jit(solution)/shard_map/ppermute | solution.py:24
  111.4 14.4 %collective-permute-start.11 = (f32[256,1,128]{2,0,1:T(8,128)S(1)}, f32[256,1,128]{2,0,1:T(8,128)S(1)}, u32[]{:S(2)}, u32[]{:S(2)}) collective-permute-start(f32[256,1,128]{2,0,1:T(8,128)S(1)} %fusion.25), channel_id=1, source_target_pairs={{252,0},{0,4},{4,8},{8,12},{12,16},{16,20},{20,24},{24,28},{28,32}... | collective-permute-start | bytes 393224 | tf_op jit(solution)/shard_map/ppermute | solution.py:24
  114.8 8.4 %collective-permute-start.4 = (bf16[256,1,128]{2,0,1:T(8,128)(2,1)S(1)}, bf16[256,1,128]{2,0,1:T(8,128)(2,1)S(1)}, u32[]{:S(2)}, u32[]{:S(2)}) collective-permute-start(bf16[256,1,128]{2,0,1:T(8,128)(2,1)S(1)} %collective-permute-done.2), channel_id=1, source_target_pairs={{0,4},{4,8},{8,12},{12,16},{16,20},{20,24},{24,28},{28,32},{32,36}... | collective-permute-start | bytes 196616 | tf_op jit(solution)/shard_map/ppermute | solution.py:18
  117.7 7.1 %collective-permute-start.5 = (bf16[256,1,128]{2,0,1:T(8,128)(2,1)S(1)}, bf16[256,1,128]{2,0,1:T(8,128)(2,1)S(1)}, u32[]{:S(2)}, u32[]{:S(2)}) collective-permute-start(bf16[256,1,128]{2,0,1:T(8,128)(2,1)S(1)} %collective-permute-done.3), channel_id=1, source_target_pairs={{0,4},{4,8},{8,12},{12,16},{16,20},{20,24},{24,28},{28,32},{32,36}... | collective-permute-start | bytes 196616 | tf_op jit(solution)/shard_map/ppermute | solution.py:18
  125.3 6.0 %collective-permute-start.8 = (f32[256,1,128]{2,0,1:T(8,128)S(1)}, f32[256,1,128]{2,0,1:T(8,128)S(1)}, u32[]{:S(2)}, u32[]{:S(2)}) collective-permute-start(f32[256,1,128]{2,0,1:T(8,128)S(1)} %add.51), channel_id=1, source_target_pairs={{252,0},{0,4},{4,8},{8,12},{12,16},{16,20},{20,24},{24,28},{28,32}... | collective-permute-start | bytes 393224 | tf_op jit(solution)/shard_map/ppermute | solution.py:24
  125.8 6.9 %collective-permute-start.12 = (f32[256,1,128]{2,0,1:T(8,128)S(1)}, f32[256,1,128]{2,0,1:T(8,128)S(1)}, u32[]{:S(2)}, u32[]{:S(2)}) collective-permute-start(f32[256,1,128]{2,0,1:T(8,128)S(1)} %add.54), channel_id=1, source_target_pairs={{252,0},{0,4},{4,8},{8,12},{12,16},{16,20},{20,24},{24,28},{28,32}... | collective-permute-start | bytes 393224 | tf_op jit(solution)/shard_map/ppermute | solution.py:24
  131.3 6.4 %collective-permute-start.9 = (bf16[256,1,128]{2,0,1:T(8,128)(2,1)S(1)}, bf16[256,1,128]{2,0,1:T(8,128)(2,1)S(1)}, u32[]{:S(2)}, u32[]{:S(2)}) collective-permute-start(bf16[256,1,128]{2,0,1:T(8,128)(2,1)S(1)} %add_convert_fusion.1), channel_id=1, source_target_pairs={{12,0},{16,4},{20,8},{24,12},{28,16},{32,20},{36,24},{40,28},{44,3... | collective-permute-start | bytes 196616 | tf_op jit(solution)/shard_map/ppermute | solution.py:24
  132.7 5.7 %collective-permute-start.13 = (bf16[256,1,128]{2,0,1:T(8,128)(2,1)S(1)}, bf16[256,1,128]{2,0,1:T(8,128)(2,1)S(1)}, u32[]{:S(2)}, u32[]{:S(2)}) collective-permute-start(bf16[256,1,128]{2,0,1:T(8,128)(2,1)S(1)} %add_convert_fusion), channel_id=1, source_target_pairs={{12,0},{16,4},{20,8},{24,12},{28,16},{32,20},{36,24},{40,28},{44,3... | collective-permute-start | bytes 196616 | tf_op jit(solution)/shard_map/ppermute | solution.py:24
Sparse Core Ops, SparseCore 0:
  9.8 63.1 all-gather.1
  76.8 89.6 reduce-scatter.1

commit v2 on v0

v2 whole, which is shorter than its diff:
```python
import jax
import jax.numpy as jnp
from jax import lax
from jax.experimental import pallas as pl
from jax.experimental.pallas import tpu as pltpu
from jax.sharding import PartitionSpec as P

HD = 128
WIN = 4
CTX = 64
CAP = 16
TOK = 256
HEADS = 8
FFT = 384
WIDTH = 1024
SLOTS = CTX * CAP
COL = 8 * CAP
SCALE = HD**-0.5
MESH = pl.DeviceIdType.MESH
F32, BF16 = jnp.float32, jnp.bfloat16


def place(ctx, offset):
    x = lax.rem(ctx // 32 + offset // 32, 2)
    y = lax.rem(lax.rem(ctx // 8, 4) + lax.rem(offset // 8, 4), 4)
    z = lax.rem(lax.rem(ctx, 8) + lax.rem(offset, 8), 8)
    return (x * 4 + y) * 8 + z


def dot(a, b):
    return jnp.dot(a, b, preferred_element_type=F32)


def aligned(index, size):
    return pl.ds(pl.multiple_of(index * size, size), size)


def kernel(
    queries, keys, values, outputs, grad_out, log_sums, block_mask, tokens, ids, probs, hidden, down,
    dq_stack, dkv, gw, gh,
    q_stack, g_stack, o_stack, q_turned, g_turned, log_rows, delta, mask_row, kv, k_turned, p_all, s_all,
    home, ret_out, ret_in,
    tok, id_rows, prob_rows, routed, received, hid, hid_all, down_here, total,
    own_part, far_part, near_out, near_in, far_out, far_in,
    in_sems, kv_sems, ret_sems, hid_sems, send_sem, recv_sems, near_sems, far_sems,
):
    ctx, tp = lax.axis_index("ctx"), lax.axis_index("tp")
    sibling = (tp // 2) * 2 + (1 - lax.rem(tp, 2))
    across = lax.rem(tp + 2, 4)
    diagonal = lax.rem(sibling + 2, 4)
    barrier = pltpu.get_barrier_semaphore()

    def greet(offset, carry):
        pl.semaphore_signal(barrier, inc=1, device_id=(place(ctx, offset), tp), device_id_type=MESH)
        return carry

    lax.fori_loop(1, CTX, greet, 0)
    for other in (sibling, across):
        pl.semaphore_signal(barrier, inc=1, device_id=(ctx, other), device_id_type=MESH)

    def fetch(index, source, target):
        copy = pltpu.make_async_copy(source, target, in_sems.at[index])
        copy.start()
        return copy

    get_ids = fetch(0, ids, id_rows)
    get_probs = fetch(1, probs, prob_rows)
    get_tokens = fetch(2, tokens, tok)
    get_hidden = fetch(3, hidden, hid)
    get_keys = fetch(4, keys, kv.at[0, 0])
    get_values = fetch(5, values, kv.at[0, 1])
    get_logs = fetch(6, log_sums, log_rows)
    get_mask = fetch(7, block_mask, mask_row)
    get_heads = []
    for index, (source, target) in enumerate(((queries, q_stack), (grad_out, g_stack), (outputs, o_stack))):
        for head in range(HEADS):
            get_heads.append(
                fetch(
                    9 + index * HEADS + head,
                    source.at[:, pl.ds(head * HD, HD)],
                    target.at[pl.ds(head * TOK, TOK)],
                )
            )
    get_down = fetch(8, down, down_here)

    get_hidden.wait()

    def turn_hidden(part, carry):
        hid_all[tp, :, aligned(part, 256)] = hid[aligned(part, 256), :].T
        return carry

    lax.fori_loop(0, SLOTS // 256, turn_hidden, 0)

    get_ids.wait()
    get_probs.wait()
    experts = lax.broadcasted_iota(jnp.int32, (CTX, TOK), 0)
    named = [id_rows[rank : rank + 1, :] == experts for rank in range(2)]
    before = (
        lax.broadcasted_iota(jnp.int32, (TOK, TOK), 0) < lax.broadcasted_iota(jnp.int32, (TOK, TOK), 1)
    ).astype(BF16)
    earlier = dot((named[0] | named[1]).astype(BF16), before)
    wanted = []
    for rank in range(2):
        slot = jnp.sum(jnp.where(named[rank], earlier, 0.0), axis=0, keepdims=True).astype(jnp.int32)
        wanted.append(id_rows[rank : rank + 1, :] * CAP + slot)
    get_tokens.wait()

    def pick(column, carry):
        slots = lax.broadcasted_iota(jnp.int32, (COL, TOK), 0) + column * COL
        chosen = [slots == wanted[rank] for rank in range(2)]
        factor = jnp.sum(
            jnp.where(chosen[0], prob_rows[0:1, :], 0.0) + jnp.where(chosen[1], prob_rows[1:2, :], 0.0),
            axis=1,
            keepdims=True,
        )
        rows = dot((chosen[0] | chosen[1]).astype(BF16), tok[...])
        routed[aligned(column, COL), :] = (rows * factor).astype(BF16)
        return carry

    lax.fori_loop(0, 8, pick, 0)
    get_keys.wait()
    get_values.wait()
    pl.semaphore_wait(barrier, CTX + 1)

    def remote(source, target, sends, receives, device):
        copy = pltpu.make_async_remote_copy(
            src_ref=source, dst_ref=target, send_sem=sends, recv_sem=receives, device_id=device, device_id_type=MESH
        )
        copy.start()
        return copy

    kv_copies = [
        remote(
            kv.at[0], kv.at[lag], kv_sems.at[0, lag - 1], kv_sems.at[1, lag - 1], (lax.rem(ctx + lag, CTX), tp)
        )
        for lag in range(1, WIN)
    ]
    hid_across = remote(hid_all.at[tp], hid_all.at[tp], hid_sems.at[0, 0], hid_sems.at[1, 0], (ctx, across))
    hid_near = remote(hid_all.at[tp], hid_all.at[tp], hid_sems.at[0, 1], hid_sems.at[1, 1], (ctx, sibling))

    def send(index, carry):
        column = lax.rem(index // 8, 2) * 4 + index // 16
        target = place(ctx, column * 8 + lax.rem(index, 8))
        remote(
            routed.at[aligned(target, CAP)],
            received.at[aligned(ctx, CAP)],
            send_sem,
            recv_sems.at[column],
            (target, tp),
        )
        return carry

    lax.fori_loop(1, CTX, send, 0)
    received[aligned(ctx, CAP), :] = routed[aligned(ctx, CAP), :]

    for copy in get_heads:
        copy.wait()
    get_logs.wait()
    get_mask.wait()

    def turn_heads(head, carry):
        rows, lanes = aligned(head, TOK), aligned(head, HD)
        q_turned[lanes, :] = q_stack[rows, :].T
        turned = g_stack[rows, :].T
        g_turned[lanes, :] = turned
        delta[pl.ds(head, 1), :] = jnp.sum(
            turned.astype(F32) * o_stack[rows, :].T.astype(F32), axis=0, keepdims=True
        )
        return carry

    lax.fori_loop(0, HEADS, turn_heads, 0)

    def attend(lag, carry):
        @pl.when(lag > 0)
        def _():
            pltpu.make_async_copy(kv.at[lag], kv.at[lag], kv_sems.at[1, lag - 1]).wait()

        lag_rows = aligned(lag, TOK)
        k_turned[:, lag_rows] = kv[lag, 0].T
        given = jnp.sum(
            jnp.where(
                lax.broadcasted_iota(jnp.int32, (1, WIN - 1), 1) == lag - 1, mask_row[...], 0
            ).astype(F32),
            axis=1,
            keepdims=True,
        )
        live = jnp.where(lag == 0, 1.0, jnp.where(ctx - lag >= 0, given, 0.0))
        key_at = lax.broadcasted_iota(jnp.int32, (TOK, TOK), 0)
        query_at = lax.broadcasted_iota(jnp.int32, (TOK, TOK), 1)
        factor = jnp.where(key_at <= query_at + lag * TOK, live, 0.0)

        def head_terms(head, carry):
            lanes = aligned(head, HD)
            scores = dot(kv[lag, 0], q_turned[lanes, :]) * SCALE
            weights = jnp.exp(scores - log_rows[pl.ds(head, 1), :]) * factor
            p_all[:, aligned(head, TOK)] = weights.astype(BF16)
            grads = dot(kv[lag, 1], g_turned[lanes, :])
            s_all[lag_rows, aligned(head, TOK)] = (weights * (grads - delta[pl.ds(head, 1), :])).astype(BF16)
            return carry

        lax.fori_loop(0, HEADS, head_terms, 0)
        key_term = dot(s_all[lag_rows, :], q_stack[...])
        value_term = dot(p_all[...], g_stack[...])

        @pl.when(lag == 0)
        def _():
            home[0] = key_term
            home[1] = value_term

        @pl.when(lag > 0)
        def _():
            ret_out[lag - 1, 0] = key_term.astype(BF16)
            ret_out[lag - 1, 1] = value_term.astype(BF16)
            remote(
                ret_out.at[lag - 1],
                ret_in.at[lag - 1],
                ret_sems.at[0, lag - 1],
                ret_sems.at[1, lag - 1],
                (lax.rem(ctx + CTX - lag, CTX), tp),
            )

        return carry

    lax.fori_loop(0, WIN, attend, 0)

    def finish_queries(head, carry):
        turned = dot(k_turned[...], s_all[:, aligned(head, TOK)]) * SCALE
        dq_stack[aligned(head, TOK), :] = turned.T.astype(BF16)
        return carry

    lax.fori_loop(0, HEADS, finish_queries, 0)
    hid_across.wait()
    hid_on = remote(hid_all.at[across], hid_all.at[across], hid_sems.at[0, 2], hid_sems.at[1, 2], (ctx, sibling))
    get_down.wait()

    def columns_of(pair):
        x, y = ctx // 32, lax.rem(ctx // 8, 4)
        there = lax.rem(y + 4 - pair, 4)
        return x * 4 + there, (1 - x) * 4 + there

    def take(pair):
        for half, column in enumerate((pair, pair + 4)):
            rows = pl.ds(0, COL - CAP) if half == 0 and isinstance(pair, int) and pair == 0 else pl.ds(0, COL)
            pltpu.make_async_copy(received.at[rows], received.at[rows], recv_sems.at[column]).wait()
        a, b = columns_of(pair)
        rows = jnp.concatenate([received[aligned(a, COL), :], received[aligned(b, COL), :]], axis=0)

        def part(owner):
            return lax.dot_general(
                down_here[aligned(owner, FFT), :], rows, (((1,), (1,)), ((), ())), preferred_element_type=F32
            )

        near_out[pair, 0] = part(diagonal).astype(BF16)
        near_out[pair, 1] = part(sibling).astype(BF16)
        remote(near_out.at[pair], near_in.at[pair], near_sems.at[0, pair], near_sems.at[1, pair], (ctx, sibling))
        far_part[...] = part(across)
        own_part[pair] = part(tp)

    def weigh(pair, first, last, final):
        a, b = columns_of(pair)

        def tile(index, carry):
            owner, inner = index // 3, lax.rem(index, 3)
            left = jnp.concatenate(
                [
                    hid_all[owner, aligned(inner, 128), aligned(a, COL)],
                    hid_all[owner, aligned(inner, 128), aligned(b, COL)],
                ],
                axis=1,
            )
            right = jnp.concatenate([received[aligned(a, COL), :], received[aligned(b, COL), :]], axis=0)
            here = aligned(index, 128)
            term = dot(left, right)
            if final:
                gw[here, :] = (total[here, :] + term).astype(BF16)
            elif isinstance(pair, int):
                total[here, :] = term
            else:
                total[here, :] = total[here, :] + term
            return carry

        lax.fori_loop(first, last, tile, 0)

    def pass_on(pair):
        pltpu.make_async_copy(near_in.at[pair], near_in.at[pair], near_sems.at[1, pair]).wait()
        far_out[pair] = (far_part[...] + near_in[pair, 0].astype(F32)).astype(BF16)
        remote(far_out.at[pair], far_in.at[pair], far_sems.at[0, pair], far_sems.at[1, pair], (ctx, across))

    def settle(pair):
        pltpu.make_async_copy(far_in.at[pair], far_in.at[pair], far_sems.at[1, pair]).wait()
        done = (own_part[pair] + near_in[pair, 1].astype(F32) + far_in[pair].astype(F32)).astype(BF16)
        a, b = columns_of(pair)
        gh[:, aligned(a, COL)] = done[:, :COL]
        gh[:, aligned(b, COL)] = done[:, COL:]

    last = 3
    take(0)
    hid_near.wait()
    hid_on.wait()
    weigh(0, 0, 12, False)
    pass_on(0)

    def middle(pair, carry):
        take(pair)
        weigh(pair, 0, 12, False)
        pass_on(pair)
        settle(pair - 1)
        return carry

    lax.fori_loop(1, last, middle, 0)

    for lag in range(1, WIN):
        pltpu.make_async_copy(ret_in.at[lag - 1], ret_in.at[lag - 1], ret_sems.at[1, lag - 1]).wait()
    for index in range(2):
        whole = home[index]
        for lag in range(1, WIN):
            whole = whole + ret_in[lag - 1, index].astype(F32)
        dkv[index] = (whole * (SCALE if index == 0 else 1.0)).astype(BF16)

    take(last)
    weigh(last, 0, 6, True)
    pass_on(last)
    weigh(last, 6, 12, True)
    settle(last - 1)
    settle(last)

    for copy in kv_copies:
        copy.wait_send()
    for lag in range(1, WIN):
        pltpu.make_async_copy(ret_out.at[lag - 1], ret_out.at[lag - 1], ret_sems.at[0, lag - 1]).wait()
    for pair in range(4):
        pltpu.make_async_copy(near_out.at[pair], near_out.at[pair], near_sems.at[0, pair]).wait()
        pltpu.make_async_copy(far_out.at[pair], far_out.at[pair], far_sems.at[0, pair]).wait()
    rows = pl.ds(0, (CTX - 1) * CAP)
    pltpu.make_async_copy(routed.at[rows], routed.at[rows], send_sem).wait()


def hand_over(dq_stack, dkv, gw, gh, grad_queries, grad_keys, grad_values, grad_weight, grad_hidden, sems):
    pairs = [
        (dq_stack.at[pl.ds(head * TOK, TOK)], grad_queries.at[:, pl.ds(head * HD, HD)]) for head in range(HEADS)
    ]
    pairs += [(dkv.at[0], grad_keys), (dkv.at[1], grad_values), (gh, grad_hidden)]
    pairs += [(gw.at[pl.ds(part * FFT, FFT)], grad_weight.at[pl.ds(part * FFT, FFT)]) for part in range(4)]
    copies = [pltpu.make_async_copy(*pair, sems.at[index]) for index, pair in enumerate(pairs)]
    for copy in copies:
        copy.start()
    for copy in copies:
        copy.wait()


def shards(
    queries,
    keys,
    values,
    outputs,
    grad_out,
    log_sums,
    block_mask,
    grad_tokens,
    expert_ids,
    route_probs,
    hidden_saved,
    down_weight,
):
    hbm = pl.BlockSpec(memory_space=pltpu.HBM)
    vmem = pltpu.VMEM
    dma = pltpu.SemaphoreType.DMA
    heads = (HEADS * TOK, HD)
    turned = (HEADS * HD, TOK)
    results = pl.pallas_call(
        kernel,
        out_shape=[
            vmem(heads, BF16),
            vmem((2, TOK, HD), BF16),
            vmem((4 * FFT, WIDTH), BF16),
            vmem((FFT, SLOTS), BF16),
        ],
        in_specs=[hbm] * 12,
        out_specs=[pl.BlockSpec(memory_space=vmem)] * 4,
        scratch_shapes=[
            vmem(heads, BF16),
            vmem(heads, BF16),
            vmem(heads, BF16),
            vmem(turned, BF16),
            vmem(turned, BF16),
            vmem((HEADS, TOK), F32),
            vmem((HEADS, TOK), F32),
            vmem((1, WIN - 1), jnp.int32),
            vmem((WIN, 2, TOK, HD), BF16),
            vmem((HD, WIN * TOK), BF16),
            vmem((TOK, HEADS * TOK), BF16),
            vmem((WIN * TOK, HEADS * TOK), BF16),
            vmem((2, TOK, HD), F32),
            vmem((WIN - 1, 2, TOK, HD), BF16),
            vmem((WIN - 1, 2, TOK, HD), BF16),
            vmem((TOK, WIDTH), BF16),
            vmem((2, TOK), jnp.int32),
            vmem((2, TOK), F32),
            vmem((SLOTS, WIDTH), BF16),
            vmem((SLOTS, WIDTH), BF16),
            vmem((SLOTS, FFT), BF16),
            vmem((4, FFT, SLOTS), BF16),
            vmem((4 * FFT, WIDTH), BF16),
            vmem((4 * FFT, WIDTH), F32),
            vmem((4, FFT, 2 * COL), F32),
            vmem((FFT, 2 * COL), F32),
            vmem((4, 2, FFT, 2 * COL), BF16),
            vmem((4, 2, FFT, 2 * COL), BF16),
            vmem((4, FFT, 2 * COL), BF16),
            vmem((4, FFT, 2 * COL), BF16),
            dma((9 + 3 * HEADS,)),
            dma((2, WIN - 1)),
            dma((2, WIN - 1)),
            dma((2, 3)),
            dma,
            dma((8,)),
            dma((2, 4)),
            dma((2, 4)),
        ],
        compiler_params=pltpu.CompilerParams(
            collective_id=0, has_side_effects=True, vmem_limit_bytes=48 * 2**20
        ),
        name="layer",
    )(
        *[
            pltpu.with_memory_space_constraint(array, pltpu.HBM)
            for array in (
                queries,
                keys,
                values,
                outputs,
                grad_out,
                log_sums,
                block_mask,
                grad_tokens,
                expert_ids.T,
                route_probs.T,
                hidden_saved[0],
                down_weight[0],
            )
        ]
    )
    grad_queries, grad_keys, grad_values, grad_weight, grad_hidden = pl.pallas_call(
        hand_over,
        out_shape=[
            jax.ShapeDtypeStruct((TOK, WIDTH), BF16),
            jax.ShapeDtypeStruct((TOK, HD), BF16),
            jax.ShapeDtypeStruct((TOK, HD), BF16),
            jax.ShapeDtypeStruct((4 * FFT, WIDTH), BF16),
            jax.ShapeDtypeStruct((FFT, SLOTS), BF16),
        ],
        in_specs=[pl.BlockSpec(memory_space=vmem)] * 4,
        out_specs=[hbm] * 5,
        scratch_shapes=[dma((HEADS + 7,))],
        compiler_params=pltpu.CompilerParams(vmem_limit_bytes=8 * 2**20),
        name="results",
    )(*[pltpu.with_memory_space_constraint(result, pltpu.VMEM) for result in results])
    return grad_queries, grad_keys, grad_values, grad_weight[None], grad_hidden[None]


def solution(mesh):
    return jax.shard_map(
        shards,
        mesh=mesh,
        in_specs=(
            P("ctx", "tp"),
            P("ctx", "tp"),
            P("ctx", "tp"),
            P("ctx", "tp"),
            P("ctx", "tp"),
            P("tp", "ctx"),
            P("ctx", None),
            P("ctx", "tp"),
            P("ctx", None),
            P("ctx", None),
            P("ctx", None, "tp"),
            P("ctx", None, "tp"),
        ),
        out_specs=(
            P("ctx", "tp"),
            P("ctx", "tp"),
            P("ctx", "tp"),
            P("ctx", None, "tp"),
            P("ctx", "tp", None),
        ),
        check_vma=False,
    )
```

time: 209 us -> 90.9 us (0.43)
  the two profiles are of different devices: /device:TPU:25 before, /device:TPU:10 now
where the time goes in v2:
time: 90.9 us; the launch traced here: 90.8 us
  Pallas kernels  90.2 us (99%)
    pallas_call x1, Pallas kernels, shards(): pl.pallas_call(kernel, out_shape=[vmem(heads, BF16), vmem((2, TOK, HD), B...  87.9 us
    pallas_call x1, Pallas kernels, shards(): pl.pallas_call(hand_over, out_shape=[jax.ShapeDtypeStruct((TOK, WIDTH), B...  2.26 us

profile of v2, /device:TPU:10, one launch (start us, length us, event | category | flops | bytes accessed | tf_op | source)
XLA Modules:
  0.0 90.8 jit_solution(12551252993356792370)
XLA Ops:
  0.6 87.9 %layer.1 = (bf16[2048,128]{1,0:T(8,128)(2,1)S(1)}, bf16[2,256,128]{2,1,0:T(8,128)(2,1)S(1)}, bf16[1536,1024]{1,0:T(8,128)(2,1)S(1)}, bf16[384,1024]{1,0:T(8,128)(2,1)S(1)}) custom-call(bf16[256,1024]{1,0:T(8,128)(2,1)} %queries.1, bf16[256,128]{1,0:T(8,128)(2,1)} %keys.1, bf16[256,128]{1,0:T(8,128)(2,1)} %values.1, bf16[256,1024]{1,0:T(8,128)(2,1)} %outputs.1, ...), custom_call_target="tpu_custom_call" | custom-call | tf_op jit(solution)/shard_map/layer/pallas_call | solution.py:370
  88.6 2.3 %results.1 = (bf16[256,1024]{1,0:T(8,128)(2,1)}, bf16[256,128]{1,0:T(8,128)(2,1)}, bf16[256,128]{1,0:T(8,128)(2,1)}, bf16[1536,1024]{1,0:T(8,128)(2,1)}, bf16[384,1024]{1,0:T(8,128)(2,1)}) custom-call(bf16[2048,128]{1,0:T(8,128)(2,1)S(1)} %get-tuple-element.14.dq_stack, bf16[2,256,128]{2,1,0:T(8,128)(2,1)S(1)} %get-tuple-element.15.dkv, ...), custom_call_target="tpu_custom_call" | custom-call | tf_op jit(solution)/shard_map/results/pallas_call | solution.py:443

commit v3 on v2

--- a/solution.py
+++ b/solution.py
@@ -83,14 +83,6 @@
             )
     get_down = fetch(8, down, down_here)
 
-    get_hidden.wait()
-
-    def turn_hidden(part, carry):
-        hid_all[tp, :, aligned(part, 256)] = hid[aligned(part, 256), :].T
-        return carry
-
-    lax.fori_loop(0, SLOTS // 256, turn_hidden, 0)
-
     get_ids.wait()
     get_probs.wait()
     experts = lax.broadcasted_iota(jnp.int32, (CTX, TOK), 0)
@@ -135,9 +127,6 @@
         )
         for lag in range(1, WIN)
     ]
-    hid_across = remote(hid_all.at[tp], hid_all.at[tp], hid_sems.at[0, 0], hid_sems.at[1, 0], (ctx, across))
-    hid_near = remote(hid_all.at[tp], hid_all.at[tp], hid_sems.at[0, 1], hid_sems.at[1, 1], (ctx, sibling))
-
     def send(index, carry):
         column = lax.rem(index // 8, 2) * 4 + index // 16
         target = place(ctx, column * 8 + lax.rem(index, 8))
@@ -152,6 +141,17 @@
 
     lax.fori_loop(1, CTX, send, 0)
     received[aligned(ctx, CAP), :] = routed[aligned(ctx, CAP), :]
+
+    get_hidden.wait()
+
+    def turn_hidden(part, carry):
+        hid_all[tp, :, aligned(part, 256)] = hid[aligned(part, 256), :].T
+        return carry
+
+    lax.fori_loop(0, SLOTS // 256, turn_hidden, 0)
+
+    hid_across = remote(hid_all.at[tp], hid_all.at[tp], hid_sems.at[0, 0], hid_sems.at[1, 0], (ctx, across))
+    hid_near = remote(hid_all.at[tp], hid_all.at[tp], hid_sems.at[0, 1], hid_sems.at[1, 1], (ctx, sibling))
 
     for copy in get_heads:
         copy.wait()
@@ -309,6 +309,12 @@
 
     lax.fori_loop(1, last, middle, 0)
 
+    take(last)
+    weigh(last, 0, 6, True)
+    pass_on(last)
+    weigh(last, 6, 12, True)
+    settle(last - 1)
+    settle(last)
     for lag in range(1, WIN):
         pltpu.make_async_copy(ret_in.at[lag - 1], ret_in.at[lag - 1], ret_sems.at[1, lag - 1]).wait()
     for index in range(2):
@@ -317,12 +323,6 @@
             whole = whole + ret_in[lag - 1, index].astype(F32)
         dkv[index] = (whole * (SCALE if index == 0 else 1.0)).astype(BF16)
 
-    take(last)
-    weigh(last, 0, 6, True)
-    pass_on(last)
-    weigh(last, 6, 12, True)
-    settle(last - 1)
-    settle(last)
 
     for copy in kv_copies:
         copy.wait_send()

time: 90.9 us -> 90.1 us (level)
  the two profiles are of different devices: /device:TPU:10 before, /device:TPU:25 now
where the time goes in v3:
time: 90.1 us; the launch traced here: 88.7 us
  Pallas kernels  88.1 us (98%)
    pallas_call x1, Pallas kernels, shards(): pl.pallas_call(kernel, out_shape=[vmem(heads, BF16), vmem((2, TOK, HD), B...  85.8 us
    pallas_call x1, Pallas kernels, shards(): pl.pallas_call(hand_over, out_shape=[jax.ShapeDtypeStruct((TOK, WIDTH), B...  2.26 us

profile of v3, /device:TPU:25, one launch (start us, length us, event | category | flops | bytes accessed | tf_op | source)
XLA Modules:
  0.0 88.7 jit_solution(16844653069950269548)
XLA Ops:
  0.6 85.8 %layer.1 = (bf16[2048,128]{1,0:T(8,128)(2,1)S(1)}, bf16[2,256,128]{2,1,0:T(8,128)(2,1)S(1)}, bf16[1536,1024]{1,0:T(8,128)(2,1)S(1)}, bf16[384,1024]{1,0:T(8,128)(2,1)S(1)}) custom-call(bf16[256,1024]{1,0:T(8,128)(2,1)} %queries.1, bf16[256,128]{1,0:T(8,128)(2,1)} %keys.1, bf16[256,128]{1,0:T(8,128)(2,1)} %values.1, bf16[256,1024]{1,0:T(8,128)(2,1)} %outputs.1, ...), custom_call_target="tpu_custom_call" | custom-call | tf_op jit(solution)/shard_map/layer/pallas_call | solution.py:370
  86.5 2.3 %results.1 = (bf16[256,1024]{1,0:T(8,128)(2,1)}, bf16[256,128]{1,0:T(8,128)(2,1)}, bf16[256,128]{1,0:T(8,128)(2,1)}, bf16[1536,1024]{1,0:T(8,128)(2,1)}, bf16[384,1024]{1,0:T(8,128)(2,1)}) custom-call(bf16[2048,128]{1,0:T(8,128)(2,1)S(1)} %get-tuple-element.14.dq_stack, bf16[2,256,128]{2,1,0:T(8,128)(2,1)S(1)} %get-tuple-element.15.dkv, ...), custom_call_target="tpu_custom_call" | custom-call | tf_op jit(solution)/shard_map/results/pallas_call | solution.py:443
